TPU v7x, 32 devices: a whole 2x2x4 slice. The times are simulated.
32 devices in a mesh: seq: 16 (over z, y, core), tp: 2 (over x).
Axes of the slice: x: 2, y: 2, z: 4, core: 2. Of those that a mesh axis runs over, the one named last changes fastest.
Arguments:
- q_raw: bfloat16 [1024, 5120], P('seq', 'tp'), may hold values from -160 to 160
- k_raw: bfloat16 [1024, 5120], P('seq', 'tp'), may hold values from -160 to 160
- v_new: bfloat16 [1024, 5120], P('seq', 'tp'), may hold values from -8 to 8
- q_gain: float32 [5120], P('tp'), may hold values from 1.5 to 3
- k_gain: float32 [5120], P('tp'), may hold values from 1 to 2
- cache_keys: bfloat16 [512, 128, 5120], P('seq', None, 'tp'), may hold values from -10 to 10
- cache_values: bfloat16 [512, 128, 5120], P('seq', None, 'tp'), may hold values from -8 to 8
- page_table: int32 [2, 256], replicated, may hold values from 0 to 511, as said below
- cached_lengths: int32 [2], replicated, may hold values from 6553 to 32768, as said below
- req_group: int32 [4], replicated, may hold values from 0 to 1, as said below
Outputs:
- attended: bfloat16 [1024, 5120], P('seq', 'tp')
Inputs may be any that keep to these rules, and one draw needn't show every extreme that they name: `page_table`: the 256 pages of group g lie on distinct slots s with (s // 16) % 2 == g; every slot holds one page. `cached_lengths`: one group's length is exactly 32768. `req_group`: exactly 2 requests belong to each group.
All inputs are finite; a program needn't handle non-finite values.
Results may differ from a plain program's by a relative error of at most 0.013.
Values may be sent and summed in bfloat16 or wider, within the bound.
A program may use at most 256 MiB of HBM per device.

v0:
```python
import math

import jax
import jax.numpy as jnp
from jax import lax
from jax.sharding import PartitionSpec as P

HDIM = 128
GROUPS = 2
NEWTOK = 256


EPSILON = 1e-06
MASKED = -1e30


def normalize(raw_rows, gain_row, sum_squares, full_width):
    values = raw_rows.astype(jnp.float32)
    return (
        values * lax.rsqrt(sum_squares[:, None] / full_width + EPSILON) * gain_row[None, :]
    ).astype(jnp.bfloat16)


def on_device(
    q_raw,
    k_raw,
    v_new,
    q_gain,
    k_gain,
    cache_keys,
    cache_values,
    page_table,
    cached_lengths,
    req_group,
):
    tok_dev, width_local = q_raw.shape
    seq_count = lax.axis_size("seq")
    full_width = width_local * lax.axis_size("tp")
    heads_local = width_local // HDIM
    page_len = cache_keys.shape[1]
    pages_dev = cache_keys.shape[0] // GROUPS
    cache_pages = page_table.shape[1]
    requests = req_group.shape[0]
    per_group = requests // GROUPS
    group_tok = per_group * NEWTOK
    seq_index = lax.axis_index("seq")
    raw_query = q_raw.astype(jnp.float32)
    raw_key = k_raw.astype(jnp.float32)
    query_sums, key_sums = lax.psum(
        (jnp.sum(raw_query * raw_query, axis=1), jnp.sum(raw_key * raw_key, axis=1)), "tp"
    )
    queries = normalize(q_raw, q_gain, query_sums, full_width)
    new_keys = normalize(k_raw, k_gain, key_sums, full_width)
    all_queries = lax.all_gather(queries, "seq", axis=0, tiled=True)
    request_ids = jnp.arange(requests, dtype=jnp.int32)
    earlier = (req_group[:, None] == req_group[None, :]) & (
        request_ids[None, :] < request_ids[:, None]
    )
    request_rank = jnp.sum(earlier.astype(jnp.int32), axis=1)
    group_ids = jnp.arange(GROUPS, dtype=jnp.int32)
    rank_ids = jnp.arange(per_group, dtype=jnp.int32)
    chosen = (req_group[None, None, :] == group_ids[:, None, None]) & (
        request_rank[None, None, :] == rank_ids[None, :, None]
    )
    members = jnp.sum(jnp.where(chosen, request_ids[None, None, :], 0), axis=2)
    token_ids = seq_index * tok_dev + jnp.arange(tok_dev, dtype=jnp.int32)
    token_request = token_ids // NEWTOK
    key_layout = cache_keys.reshape(GROUPS, pages_dev * page_len, heads_local, HDIM)
    value_layout = cache_values.reshape(GROUPS, pages_dev * page_len, heads_local, HDIM)
    own_keys = new_keys.reshape(tok_dev, heads_local, HDIM)
    own_values = v_new.reshape(tok_dev, heads_local, HDIM)
    factor = 1.0 / math.sqrt(HDIM)
    offsets = jnp.arange(page_len, dtype=jnp.int32)
    page_ids = jnp.arange(cache_pages, dtype=jnp.int32)
    token_offsets = jnp.arange(NEWTOK, dtype=jnp.int32)
    block_rows = math.gcd(group_tok, 512)
    num_blocks = group_tok // block_rows
    pieces = []
    for group_id in range(GROUPS):
        local_slots = (
            seq_index * (GROUPS * pages_dev)
            + group_id * pages_dev
            + jnp.arange(pages_dev, dtype=jnp.int32)
        )
        matches = page_table[group_id][None, :] == local_slots[:, None]
        logical = jnp.sum(jnp.where(matches, page_ids[None, :], 0), axis=1)
        positions = (logical[:, None] * page_len + offsets[None, :]).reshape(-1)
        usable = positions < cached_lengths[group_id]
        keys_all = jnp.concatenate([key_layout[group_id], own_keys], axis=0)
        values_all = jnp.concatenate([value_layout[group_id], own_values], axis=0)
        query_rows = (members[group_id][:, None] * NEWTOK + token_offsets[None, :]).reshape(-1)
        row_request = jnp.repeat(members[group_id], NEWTOK)
        picked = jnp.take(all_queries, query_rows, axis=0).reshape(
            num_blocks, block_rows, heads_local, HDIM
        )
        picked_request = row_request.reshape(num_blocks, block_rows)

        def attend(operands):
            block_query, block_request = operands
            cached_allowed = jnp.broadcast_to(usable[None, :], (block_rows, usable.shape[0]))
            allowed = jnp.concatenate(
                [cached_allowed, block_request[:, None] == token_request[None, :]], axis=1
            )
            scores = (
                jnp.einsum(
                    "qhd,khd->hqk", block_query, keys_all, preferred_element_type=jnp.float32
                )
                * factor
            )
            scores = jnp.where(allowed[None], scores, MASKED)
            row_top = jnp.max(scores, axis=2)
            weights = jnp.where(allowed[None], jnp.exp(scores - row_top[:, :, None]), 0.0)
            totals = jnp.sum(weights, axis=2)
            mixture = jnp.einsum(
                "hqk,khd->qhd",
                weights.astype(jnp.bfloat16),
                values_all,
                preferred_element_type=jnp.float32,
            )
            return (
                mixture.reshape(block_rows, width_local),
                jnp.transpose(row_top),
                jnp.transpose(totals),
            )

        mixture, row_top, totals = lax.map(attend, (picked, picked_request))
        pieces.append(
            (
                mixture.reshape(group_tok, width_local),
                row_top.reshape(group_tok, heads_local),
                totals.reshape(group_tok, heads_local),
            )
        )
    joined_mix = jnp.concatenate([element[0] for element in pieces], axis=0)
    joined_top = jnp.concatenate([element[1] for element in pieces], axis=0)
    joined_totals = jnp.concatenate([element[2] for element in pieces], axis=0)
    request_base = req_group * group_tok + request_rank * NEWTOK
    placement_rows = (request_base[:, None] + token_offsets[None, :]).reshape(-1)
    token_mix = jnp.take(joined_mix, placement_rows, axis=0)
    token_top = jnp.take(joined_top, placement_rows, axis=0)
    token_totals = jnp.take(joined_totals, placement_rows, axis=0)
    source_mix, source_top, source_totals = (
        lax.all_to_all(
            token_mix.reshape(seq_count, tok_dev, width_local),
            "seq",
            split_axis=0,
            concat_axis=0,
            tiled=True,
        ),
        lax.all_to_all(
            token_top.reshape(seq_count, tok_dev, heads_local),
            "seq",
            split_axis=0,
            concat_axis=0,
            tiled=True,
        ),
        lax.all_to_all(
            token_totals.reshape(seq_count, tok_dev, heads_local),
            "seq",
            split_axis=0,
            concat_axis=0,
            tiled=True,
        ),
    )
    overall = jnp.max(source_top, axis=0)
    scaling = jnp.exp(source_top - overall[None])
    numerator = jnp.sum(
        source_mix.reshape(seq_count, tok_dev, heads_local, HDIM) * scaling[..., None], axis=0
    )
    denominator = jnp.sum(source_totals * scaling, axis=0)
    return (numerator / denominator[..., None]).reshape(tok_dev, width_local).astype(jnp.bfloat16)


def solution(mesh):
    return jax.shard_map(
        on_device,
        mesh=mesh,
        in_specs=(
            P("seq", "tp"),
            P("seq", "tp"),
            P("seq", "tp"),
            P("tp"),
            P("tp"),
            P("seq", None, "tp"),
            P("seq", None, "tp"),
            P(),
            P(),
            P(),
        ),
        out_specs=P("seq", "tp"),
        check_vma=False,
    )
```

profile of v0, /device:TPU:13, one launch (start us, length us, event | category | flops | bytes accessed | tf_op | source)
XLA Modules:
  0.0 731.9 jit_solution(1602742204029322264)
XLA Ops:
  20.5 16.3 %fusion.44 = (bf16[16,128,2560]{2,1,0:T(8,128)(2,1)}, bf16[16,128,2560]{2,1,0:T(8,128)(2,1)}) fusion(bf16[32,128,2560]{2,1,0:T(8,128)(2,1)} %param.19), kind=kLoop, calls=%fused_computation.118 | loop fusion | bytes 41943040 | tf_op jit(solution)/shard_map/slice | solution.py:89
  36.9 18.5 %reshape.333 = bf16[2048,20,128]{2,1,0:T(8,128)(2,1)} reshape(bf16[16,128,2560]{2,1,0:T(8,128)(2,1)} %get-tuple-element.61) | data formatting | bytes 20971520 | tf_op jit(solution)/shard_map/squeeze | solution.py:89
  55.4 11.5 %copy.89 = bf16[2048,20,128]{2,0,1:T(8,128)(2,1)} copy(bf16[2048,20,128]{2,1,0:T(8,128)(2,1)} %reshape.333) | data formatting | bytes 20971520 | tf_op jit(solution)/shard_map/squeeze | solution.py:89
  66.8 18.5 %reshape.335 = bf16[2048,20,128]{2,1,0:T(8,128)(2,1)} reshape(bf16[16,128,2560]{2,1,0:T(8,128)(2,1)} %get-tuple-element.62) | data formatting | bytes 20971520 | tf_op jit(solution)/shard_map/squeeze | solution.py:89
  85.4 11.2 %copy.97 = bf16[2048,20,128]{2,0,1:T(8,128)(2,1)} copy(bf16[2048,20,128]{2,1,0:T(8,128)(2,1)} %reshape.335) | data formatting | bytes 20971520 | tf_op jit(solution)/shard_map/squeeze | solution.py:89
  96.6 16.3 %fusion.43 = (bf16[16,128,2560]{2,1,0:T(8,128)(2,1)}, bf16[16,128,2560]{2,1,0:T(8,128)(2,1)}) fusion(bf16[32,128,2560]{2,1,0:T(8,128)(2,1)} %param.20), kind=kLoop, calls=%fused_computation.117 | loop fusion | bytes 41943040 | tf_op jit(solution)/shard_map/slice | solution.py:90
  112.9 18.4 %reshape.332 = bf16[2048,20,128]{2,1,0:T(8,128)(2,1)} reshape(bf16[16,128,2560]{2,1,0:T(8,128)(2,1)} %get-tuple-element.49) | data formatting | bytes 20971520 | tf_op jit(solution)/shard_map/squeeze | solution.py:90
  131.3 11.2 %copy.85 = bf16[2048,20,128]{2,0,1:T(8,128)(2,1)} copy(bf16[2048,20,128]{2,1,0:T(8,128)(2,1)} %reshape.332) | data formatting | bytes 20971520 | tf_op jit(solution)/shard_map/squeeze | solution.py:90
  142.5 18.4 %reshape.334 = bf16[2048,20,128]{2,1,0:T(8,128)(2,1)} reshape(bf16[16,128,2560]{2,1,0:T(8,128)(2,1)} %get-tuple-element.60) | data formatting | bytes 20971520 | tf_op jit(solution)/shard_map/squeeze | solution.py:90
  160.9 11.3 %copy.93 = bf16[2048,20,128]{2,0,1:T(8,128)(2,1)} copy(bf16[2048,20,128]{2,1,0:T(8,128)(2,1)} %reshape.334) | data formatting | bytes 20971520 | tf_op jit(solution)/shard_map/squeeze | solution.py:90
  180.7 8.4 %gather_fusion.2 = bf16[512,2560]{1,0:T(8,128)(2,1)S(1)} fusion(bf16[1024,2560]{1,0:T(8,128)(2,1)} %all-gather.2.cloned.1.call-done, s32[1024]{0:T(1024)S(1)} %pad_clamp_fusion), kind=kCustom, calls=%fused_computation.2.clone | custom fusion | bytes 5244928 | tf_op jit(solution)/shard_map/jit(_take)/gather | solution.py:93
  195.3 8.6 %gather_fusion.1 = bf16[512,2560]{1,0:T(8,128)(2,1)S(1)} fusion(bf16[1024,2560]{1,0:T(8,128)(2,1)} %all-gather.2.cloned.1.call-done, s32[1024]{0:T(1024)S(1)} %pad_clamp_fusion.1), kind=kCustom, calls=%fused_computation.clone | custom fusion | bytes 5244928 | tf_op jit(solution)/shard_map/jit(_take)/gather | solution.py:93
  210.1 35.8 %fusion.1 = (f32[20,512]{1,0:T(8,128)S(1)}, f32[20,512,2112]{1,2,0:T(8,128)}) fusion(pred[512,2112]{0,1:T(8,128)(4,1)} %pad_add_fusion.1, bf16[512,20,128]{0,2,1:T(8,128)(2,1)} %bitcast.81, bf16[64,20,128]{2,0,1:T(8,128)(2,1)S(1)} %copy_bitcast_fusion, bf16[2048,20,128]{2,0,1:T(8,128)(2,1)} %copy.97), kind=kOutput, calls=%fused_computation.10 | convolution fusion | flops 5622978560 | bytes 101064704 | tf_op jit(solution)/shard_map/while/body/eval_jaxpr/qhd,khd->hqk/dot_general | solution.py:105
  246.0 27.9 %fusion.4 = f32[20,512]{1,0:T(8,128)} fusion(f32[20,512,2112]{1,2,0:T(8,128)} %get-tuple-element.90, f32[20,512]{1,0:T(8,128)S(1)} %get-tuple-element.89, pred[512,2112]{0,1:T(8,128)(4,1)S(1)} %copy-done.3), kind=kLoop, calls=%fused_computation.13 | loop fusion | flops 108124160 | bytes 87670784 | tf_op jit(solution)/shard_map/while/body/eval_jaxpr/reduce_sum | solution.py:113
  273.9 39.4 %fusion.6 = f32[20,128,512]{2,1,0:T(8,128)} fusion(f32[20,512,2112]{1,2,0:T(8,128)} %get-tuple-element.90, f32[20,512]{1,0:T(8,128)S(1)} %get-tuple-element.89, pred[512,2112]{0,1:T(8,128)(4,1)S(1)} %copy-done.3, bf16[64,20,128]{2,0,1:T(8,128)(2,1)S(1)} %copy_bitcast_fusion.1, bf16[2048,20,128]{2,0,1:T(8,128)(2,1)} %copy.93), kind=kOutput, calls=%fused_computation.15 | convolution fusion | flops 5666242560 | bytes 103686144 | tf_op jit(solution)/shard_map/while/body/eval_jaxpr/hqk,khd->qhd/dot_general | solution.py:114
  319.2 35.5 %fusion = (f32[20,512]{1,0:T(8,128)S(1)}, f32[20,512,2112]{1,2,0:T(8,128)}) fusion(pred[512,2112]{0,1:T(8,128)(4,1)S(1)} %copy-done.2, bf16[512,20,128]{0,2,1:T(8,128)(2,1)} %bitcast.80, bf16[64,20,128]{2,0,1:T(8,128)(2,1)S(1)} %copy_bitcast_fusion, bf16[2048,20,128]{2,0,1:T(8,128)(2,1)} %copy.89), kind=kOutput, calls=%fused_computation.9 | convolution fusion | flops 5622978560 | bytes 101064704 | tf_op jit(solution)/shard_map/while/body/eval_jaxpr/qhd,khd->hqk/dot_general | solution.py:105
  354.8 27.3 %fusion.2 = f32[20,512]{1,0:T(8,128)S(1)} fusion(f32[20,512,2112]{1,2,0:T(8,128)} %get-tuple-element.92, f32[20,512]{1,0:T(8,128)S(1)} %get-tuple-element.91, pred[512,2112]{0,1:T(8,128)(4,1)S(1)} %copy-done.2), kind=kLoop, calls=%fused_computation.11 | loop fusion | flops 108124160 | bytes 87670784 | tf_op jit(solution)/shard_map/while/body/eval_jaxpr/reduce_sum | solution.py:113
  382.1 39.2 %fusion.8 = f32[20,128,512]{2,1,0:T(8,128)} fusion(f32[20,512,2112]{1,2,0:T(8,128)} %get-tuple-element.92, f32[20,512]{1,0:T(8,128)S(1)} %get-tuple-element.91, pred[512,2112]{0,1:T(8,128)(4,1)S(1)} %copy-done.2, bf16[64,20,128]{2,0,1:T(8,128)(2,1)S(1)} %copy_bitcast_fusion.1, bf16[2048,20,128]{2,0,1:T(8,128)(2,1)} %copy.85), kind=kOutput, calls=%fused_computation.16 | convolution fusion | flops 5666242560 | bytes 103686144 | tf_op jit(solution)/shard_map/while/body/eval_jaxpr/hqk,khd->qhd/dot_general | solution.py:114
  442.4 8.8 %pad_maximum_fusion.8 = f32[1024,2560]{1,0:T(8,128)} fusion(f32[512,2560]{1,0:T(8,128)} %copy.101, f32[512,2560]{1,0:T(8,128)} %copy.100), kind=kLoop, calls=%fused_computation.29 | loop fusion | flops 2621440 | bytes 20971520 | tf_op jit(solution)/shard_map/concatenate | solution.py:134
  452.1 14.3 %gather_fusion = f32[1024,2560]{1,0:T(8,128)} fusion(f32[1024,2560]{1,0:T(8,128)} %pad_maximum_fusion.8, s32[1024]{0:T(1024)S(1)} %copy-done.7), kind=kCustom, calls=%fused_computation.4 | custom fusion | bytes 20975616 | tf_op jit(solution)/shard_map/jit(_take)/gather | solution.py:139
  472.5 8.7 %broadcast_select_fusion = f32[16,64,2560]{2,1,0:T(8,128)} fusion(f32[16,64,2560]{2,1,0:T(8,128)} %bitcast.76, pred[16,64]{1,0:T(8,128)(4,1)S(1)} %copy-done.9), kind=kLoop, calls=%fused_computation.31 | loop fusion | flops 2621440 | bytes 20972544 | tf_op jit(solution)/shard_map/jit(_take)/select_n | solution.py:139
  497.5 13.0 %mul.126 = f32[16,64,2560]{2,1,0:T(8,128)} reshape(f32[16,64,20,128]{3,2,1,0:T(8,128)} %mul.125) | data formatting | bytes 20971520 | tf_op jit(solution)/shard_map/mul | solution.py:168
  510.5 204.2 %all-to-all-done = f32[16,64,2560]{2,1,0:T(8,128)} async-done(((f32[16,64,2560]{2,1,0:T(8,128)}), f32[16,64,2560]{2,1,0:T(8,128)}, u32[]{:S(2)}, u32[]{:S(2)}) %all-to-all-start) | async-done | bytes 10485792 | tf_op jit(solution)/shard_map/all_to_all | solution.py:143
  714.7 9.0 %multiply_reduce_fusion = f32[64,2560]{1,0:T(8,128)S(1)} fusion(f32[16,64,2560]{2,1,0:T(8,128)} %all-to-all-done, f32[16,64,2560]{2,1,0:T(8,128)} %mul.126), kind=kLoop, calls=%fused_computation.30 | loop fusion | flops 5079040 | bytes 21626880 | tf_op jit(solution)/shard_map/reduce_sum | solution.py:167
  (114 shorter events, 86.0 us)
Async XLA Ops:
  6.5 168.3 %copy-start = (bf16[64,2560]{1,0:T(8,128)(2,1)S(1)}, bf16[64,2560]{1,0:T(8,128)(2,1)}, u32[]{:S(2)}) copy-start(bf16[64,2560]{1,0:T(8,128)(2,1)} %param.16) | copy-start | bytes 983044
  6.5 174.2 %all-gather.2.cloned.1.call-start = ((), (), s32[]{:S(2)}) async-start(), calls=%async_computation.3 | async-start | bytes 5570560 | tf_op jit(solution)/shard_map/all_gather | solution.py:54
  160.9 14.0 %copy-start.4 = (bf16[64,2560]{1,0:T(8,128)(2,1)S(1)}, bf16[64,2560]{1,0:T(8,128)(2,1)}, u32[]{:S(2)}) copy-start(bf16[64,2560]{1,0:T(8,128)(2,1)} %param.15) | copy-start | bytes 983044
  160.9 14.1 %copy-start.8 = (f32[2560]{0:T(1024)S(1)}, f32[2560]{0:T(1024)}, u32[]{:S(2)}) copy-start(f32[2560]{0:T(1024)} %param.18) | copy-start | bytes 30724
  210.1 35.8 %copy-start.3 = (pred[512,2112]{0,1:T(8,128)(4,1)S(1)}, pred[512,2112]{0,1:T(8,128)(4,1)}, u32[]{:S(2)}) copy-start(pred[512,2112]{0,1:T(8,128)(4,1)} %pad_add_fusion.1) | copy-start | bytes 3244036
  273.9 45.3 %copy-start.2 = (pred[512,2112]{0,1:T(8,128)(4,1)S(1)}, pred[512,2112]{0,1:T(8,128)(4,1)}, u32[]{:S(2)}) copy-start(pred[512,2112]{0,1:T(8,128)(4,1)} %pad_add_fusion) | copy-start | bytes 3244036
  421.3 6.1 copy-start.5
  421.3 6.4 copy-start.6
  421.3 12.0 %copy-start.10 = (pred[1024]{0:T(1024)(128)(4,1)S(1)}, pred[1024]{0:T(1024)(128)(4,1)}, u32[]{:S(2)}) copy-start(pred[1024]{0:T(1024)(128)(4,1)} %compare_and_fusion.1) | copy-start | bytes 3076
  434.6 31.9 %all-to-all-start.2 = ((f32[16,1,1280]{2,1,0:T(1,128)}), f32[16,1,1280]{2,1,0:T(1,128)S(1)}, u32[]{:S(2)}, u32[]{:S(2)}) async-start(f32[16,1,1280]{2,1,0:T(1,128)} %reshape.340), calls=%async_computation.2 | async-start | bytes 163840 | tf_op jit(solution)/shard_map/all_to_all | solution.py:157
  442.4 9.8 %copy-start.7 = (s32[1024]{0:T(1024)S(1)}, s32[1024]{0:T(1024)}, u32[]{:S(2)}) copy-start(s32[1024]{0:T(1024)} %broadcast_clamp_fusion) | copy-start | bytes 12292
  452.1 20.3 %copy-start.9 = (pred[16,64]{1,0:T(8,128)(4,1)S(1)}, pred[16,64]{1,0:T(8,128)(4,1)}, u32[]{:S(2)}) copy-start(pred[16,64]{1,0:T(8,128)(4,1)} %compare_and_fusion) | copy-start | bytes 3076
  466.5 14.7 %all-to-all-start.1 = ((f32[16,1,1280]{2,1,0:T(1,128)}), f32[16,1,1280]{2,1,0:T(1,128)S(1)}, u32[]{:S(2)}, u32[]{:S(2)}) async-start(f32[16,1,1280]{2,1,0:T(1,128)} %reshape.338), calls=%async_computation.1 | async-start | bytes 163840 | tf_op jit(solution)/shard_map/all_to_all | solution.py:150
  481.1 233.5 %all-to-all-start = ((f32[16,64,2560]{2,1,0:T(8,128)}), f32[16,64,2560]{2,1,0:T(8,128)}, u32[]{:S(2)}, u32[]{:S(2)}) async-start(f32[16,64,2560]{2,1,0:T(8,128)} %broadcast_select_fusion), calls=%async_computation | async-start | bytes 20971520 | tf_op jit(solution)/shard_map/all_to_all | solution.py:143
  497.5 227.4 %copy-start.1 = (bf16[64,2560]{1,0:T(8,128)(2,1)S(1)}, bf16[64,2560]{1,0:T(8,128)(2,1)}, u32[]{:S(2)}) copy-start(bf16[64,2560]{1,0:T(8,128)(2,1)} %param.16) | copy-start | bytes 983044
Sparse Core Ops, SparseCore 0:
  13.7 57.7 all-gather.1
where the time goes:
time: 744 us; the launch traced here: 732 us
  local copies, waits for them, and re-layouts  236 us (32%)
  waiting for transfers between devices  204 us (27%)
  matrix products  150 us (20%)
  other arithmetic  104 us (14%)
  starting transfers between devices  20.1 us (3%)
  between operations  13.9 us (2%)
    all_to_all x1, waiting for transfers between devices, on_device(): lax.all_to_all(token_mix.reshape(seq_count, tok_dev, width_local), 'seq',...  204 us
    dot_general x2, matrix products, attend(): jnp.einsum('hqk,khd->qhd', weights.astype(jnp.bfloat16), values_all, pref...  78.7 us
    dot_general x2, matrix products, attend(): jnp.einsum('qhd,khd->hqk', block_query, keys_all, preferred_element_type=...  71.4 us
    squeeze x4, local copies, waits for them, and re-layouts, on_device(): keys_all = jnp.concatenate([key_layout[group_id], own_keys], axis=0)  59.7 us
    squeeze x4, local copies, waits for them, and re-layouts, on_device(): values_all = jnp.concatenate([value_layout[group_id], own_values], axis=0)  59.3 us
    reduce_sum x2, other arithmetic, attend(): totals = jnp.sum(weights, axis=2)  55.3 us
    mul x2, local copies, waits for them, and re-layouts, on_device(): source_mix.reshape(seq_count, tok_dev, heads_local, HDIM)  20.1 us
    gather x2, local copies, waits for them, and re-layouts, on_device(): jnp.take(all_queries, query_rows, axis=0)  17 us
  transfers between devices with their start and end apart: 4, of which 1 were waited for; matrix products, arithmetic and copies ran while one was open for 30% of the time, Pallas kernels for 0%

commit v1 on v0

v1 whole, which is shorter than its diff:
```python
import functools
import math

import jax
import jax.numpy as jnp
from jax import lax
from jax.experimental import pallas as pl
from jax.experimental.pallas import tpu as pltpu
from jax.sharding import PartitionSpec as P

HDIM = 128
GROUPS = 2
NEWTOK = 256
EPSILON = 1e-06
MASKED = -1e30
FACTOR = math.log2(math.e) / math.sqrt(HDIM)
BLOCK = 4


def normalize(raw_rows, gain_row, sum_squares, full_width):
    values = raw_rows.astype(jnp.float32)
    return (
        values * lax.rsqrt(sum_squares[:, None] / full_width + EPSILON) * gain_row[None, :]
    ).astype(jnp.bfloat16)


def attend_kernel(
    per_group,
    head_block,
    order_ref,
    limit_ref,
    count_ref,
    member_ref,
    own_ref,
    q_ref,
    k_ref,
    v_ref,
    nk_ref,
    nv_ref,
    o_ref,
    lse_ref,
    top_ref,
    total_ref,
    acc_ref,
):
    group = pl.program_id(1)
    page_len = k_ref.shape[2]
    own_rank = own_ref[group]
    full_pages = count_ref[group, 0]
    valid_pages = count_ref[group, 1]
    members = [member_ref[group, i] for i in range(per_group)]
    lanes = per_group * NEWTOK
    heads = [slice(j * HDIM, (j + 1) * HDIM) for j in range(head_block)]

    def query(j):
        return jnp.concatenate([q_ref[m, :, heads[j]] for m in members], axis=0)

    def scores_of(keys, j):
        return lax.dot_general(
            keys, query(j), (((1,), (1,)), ((), ())), preferred_element_type=jnp.float32
        )

    def mix_of(values, weights):
        return lax.dot_general(
            values,
            weights.astype(jnp.bfloat16),
            (((0,), (0,)), ((), ())),
            preferred_element_type=jnp.float32,
        )

    mine = lax.broadcasted_iota(jnp.int32, (1, lanes), 1) // NEWTOK == own_rank
    for j in range(head_block):
        scores = jnp.where(mine, scores_of(nk_ref[:, heads[j]], j), MASKED)
        top = jnp.max(scores, axis=0, keepdims=True)
        weights = jnp.where(mine, jnp.exp2(scores * FACTOR - top * FACTOR), 0.0)
        top_ref[j] = top
        total_ref[j] = jnp.sum(weights, axis=0, keepdims=True)
        acc_ref[j] = mix_of(nv_ref[:, heads[j]], weights)

    def update(pages, masked, limit):
        for j in range(head_block):
            keys = jnp.concatenate([k_ref[0, p, :, heads[j]] for p in pages], axis=0)
            values = jnp.concatenate([v_ref[0, p, :, heads[j]] for p in pages], axis=0)
            scores = scores_of(keys, j)
            if masked:
                allowed = lax.broadcasted_iota(jnp.int32, scores.shape, 0) < limit
                scores = jnp.where(allowed, scores, MASKED)
            before = top_ref[j]
            top = jnp.maximum(before, jnp.max(scores, axis=0, keepdims=True))
            weights = jnp.exp2(scores * FACTOR - top * FACTOR)
            fade = jnp.exp2((before - top) * FACTOR)
            top_ref[j] = top
            total_ref[j] = total_ref[j] * fade + jnp.sum(weights, axis=0, keepdims=True)
            acc_ref[j] = acc_ref[j] * fade + mix_of(values, weights)

    blocks = full_pages // BLOCK

    def full_step(b, _):
        update([order_ref[group, b * BLOCK + i] for i in range(BLOCK)], False, None)
        return 0

    def tail_step(p, _):
        update([order_ref[group, p]], True, limit_ref[group, p])
        return 0

    lax.fori_loop(0, blocks, full_step, 0)
    lax.fori_loop(blocks * BLOCK, valid_pages, tail_step, 0)

    for j in range(head_block):
        total = total_ref[j]
        some = total > 0.0
        inverse = 1.0 / jnp.where(some, total, 1.0)
        lse = jnp.where(some, top_ref[j] * FACTOR + jnp.log2(jnp.where(some, total, 1.0)), MASKED)
        part = (acc_ref[j] * inverse).T.astype(jnp.bfloat16)
        for i, m in enumerate(members):
            o_ref[m, :, heads[j]] = part[i * NEWTOK : (i + 1) * NEWTOK]
            lse_ref[0, j, pl.ds(m, 1), :] = lse[:, i * NEWTOK : (i + 1) * NEWTOK]


def attend(all_queries, cache_keys, cache_values, new_keys, v_new, order, limit, count, members, own):
    tokens, width = all_queries.shape
    requests = tokens // NEWTOK
    per_group = requests // GROUPS
    heads = width // HDIM
    head_block = 2 if heads % 2 == 0 else 1
    head_steps = heads // head_block
    pages = cache_keys.shape[0] // GROUPS
    page_len = cache_keys.shape[1]
    tok_dev = new_keys.shape[0]
    lanes = per_group * NEWTOK
    wide = head_block * HDIM
    keys = cache_keys.reshape(GROUPS, pages, page_len, width)
    values = cache_values.reshape(GROUPS, pages, page_len, width)
    token_spec = pl.BlockSpec((requests, NEWTOK, wide), lambda h, g, *_: (0, 0, h))
    cache_spec = pl.BlockSpec((1, pages, page_len, wide), lambda h, g, *_: (g, 0, 0, h))
    own_spec = pl.BlockSpec((tok_dev, wide), lambda h, g, *_: (0, h))
    part, lse = pl.pallas_call(
        functools.partial(attend_kernel, per_group, head_block),
        out_shape=(
            jax.ShapeDtypeStruct((requests, NEWTOK, width), jnp.bfloat16),
            jax.ShapeDtypeStruct((head_steps, head_block, requests, NEWTOK), jnp.float32),
        ),
        grid_spec=pltpu.PrefetchScalarGridSpec(
            num_scalar_prefetch=5,
            grid=(head_steps, GROUPS),
            in_specs=[token_spec, cache_spec, cache_spec, own_spec, own_spec],
            out_specs=(
                token_spec,
                pl.BlockSpec((1, head_block, requests, NEWTOK), lambda h, g, *_: (h, 0, 0, 0)),
            ),
            scratch_shapes=[
                pltpu.VMEM((head_block, 1, lanes), jnp.float32),
                pltpu.VMEM((head_block, 1, lanes), jnp.float32),
                pltpu.VMEM((head_block, HDIM, lanes), jnp.float32),
            ],
        ),
        compiler_params=pltpu.CompilerParams(
            dimension_semantics=("arbitrary", "arbitrary"), vmem_limit_bytes=48 * 1024 * 1024
        ),
        name="attend",
    )(
        order,
        limit,
        count,
        members,
        own,
        all_queries.reshape(requests, NEWTOK, width),
        keys,
        values,
        new_keys,
        v_new,
    )
    return part.reshape(tokens, width), lse.reshape(heads, tokens)


def plan_pages(page_table, cached_lengths, req_group, seq_index, pages_dev, page_len, tok_dev):
    requests = req_group.shape[0]
    per_group = requests // GROUPS
    cache_pages = page_table.shape[1]
    ids = jnp.arange(requests, dtype=jnp.int32)
    same = req_group[:, None] == req_group[None, :]
    rank = jnp.sum((same & (ids[None, :] < ids[:, None])).astype(jnp.int32), axis=1)
    groups = jnp.arange(GROUPS, dtype=jnp.int32)
    chosen = (req_group[None, None, :] == groups[:, None, None]) & (
        rank[None, None, :] == jnp.arange(per_group, dtype=jnp.int32)[None, :, None]
    )
    members = jnp.sum(jnp.where(chosen, ids[None, None, :], 0), axis=2)
    own_request = seq_index * tok_dev // NEWTOK
    is_own = members == own_request
    own = jnp.sum(jnp.where(is_own, jnp.arange(per_group, dtype=jnp.int32)[None] + 1, 0), axis=1) - 1
    local = jnp.arange(pages_dev, dtype=jnp.int32)
    slots = seq_index * (GROUPS * pages_dev) + groups[:, None] * pages_dev + local[None, :]
    hits = page_table[:, None, :] == slots[:, :, None]
    logical = jnp.sum(
        jnp.where(hits, jnp.arange(cache_pages, dtype=jnp.int32)[None, None, :], 0), axis=2
    )
    limits = jnp.clip(cached_lengths[:, None] - logical * page_len, 0, page_len)
    kind = jnp.where(limits == page_len, 0, jnp.where(limits > 0, 1, 2))
    key = kind * pages_dev + local[None, :]
    place = jnp.sum((key[:, None, :] < key[:, :, None]).astype(jnp.int32), axis=2)
    at = place[:, None, :] == local[None, :, None]
    order = jnp.sum(jnp.where(at, local[None, None, :], 0), axis=2)
    limit = jnp.sum(jnp.where(at, limits[:, None, :], 0), axis=2)
    count = jnp.stack(
        [jnp.sum((kind == 0).astype(jnp.int32), axis=1), jnp.sum((kind < 2).astype(jnp.int32), axis=1)],
        axis=1,
    )
    return order, limit, count, members, own


def on_device(
    q_raw,
    k_raw,
    v_new,
    q_gain,
    k_gain,
    cache_keys,
    cache_values,
    page_table,
    cached_lengths,
    req_group,
):
    tok_dev, width = q_raw.shape
    seq_count = lax.axis_size("seq")
    full_width = width * lax.axis_size("tp")
    heads = width // HDIM
    seq_index = lax.axis_index("seq")
    raw_query = q_raw.astype(jnp.float32)
    raw_key = k_raw.astype(jnp.float32)
    query_sums, key_sums = lax.psum(
        (jnp.sum(raw_query * raw_query, axis=1), jnp.sum(raw_key * raw_key, axis=1)), "tp"
    )
    queries = normalize(q_raw, q_gain, query_sums, full_width)
    new_keys = normalize(k_raw, k_gain, key_sums, full_width)
    all_queries = lax.all_gather(queries, "seq", axis=0, tiled=True)
    plan = plan_pages(
        page_table,
        cached_lengths,
        req_group,
        seq_index,
        cache_keys.shape[0] // GROUPS,
        cache_keys.shape[1],
        tok_dev,
    )
    part, lse = attend(all_queries, cache_keys, cache_values, new_keys, v_new, *plan)
    source_part = lax.all_to_all(
        part.reshape(seq_count, tok_dev, width), "seq", split_axis=0, concat_axis=0, tiled=True
    )
    source_lse = lax.all_to_all(
        lse.T.reshape(seq_count, tok_dev, heads), "seq", split_axis=0, concat_axis=0, tiled=True
    )
    overall = jnp.max(source_lse, axis=0)
    scaling = jnp.exp2(source_lse - overall[None])
    scaling = scaling / jnp.sum(scaling, axis=0)[None]
    mixed = jnp.sum(
        source_part.astype(jnp.float32)
        * jnp.repeat(scaling, HDIM, axis=2),
        axis=0,
    )
    return mixed.astype(jnp.bfloat16)


def solution(mesh):
    return jax.shard_map(
        on_device,
        mesh=mesh,
        in_specs=(
            P("seq", "tp"),
            P("seq", "tp"),
            P("seq", "tp"),
            P("tp"),
            P("tp"),
            P("seq", None, "tp"),
            P("seq", None, "tp"),
            P(),
            P(),
            P(),
        ),
        out_specs=P("seq", "tp"),
        check_vma=False,
    )
```

time: 744 us -> 322 us (0.43); the launches traced: 732 us -> 321 us
  local copies, waits for them, and re-layouts: 236 us -> 24.6 us
  matrix products: 150 us -> 0 us
  Pallas kernels: 0 us -> 99.1 us
  other arithmetic: 104 us -> 17.2 us
  waiting for transfers between devices: 204 us -> 146 us
  starting transfers between devices: 20.1 us -> 7.17 us
  blocking collectives: 3.79 us -> 13.9 us
    dot_general x4 -> x0, matrix products: 150 us -> none  [the longest x2 78.7 us: attend(): jnp.einsum('hqk,khd->qhd', weights.astype(jnp.bfloat16), values_all, pref...]
    squeeze x9 -> x0, local copies, waits for them, and re-layouts: 119 us -> none  [the longest x4 59.7 us: on_device(): keys_all = jnp.concatenate([key_layout[group_id], own_keys], axis=0)]
    all_to_all x3 -> x1, waiting for transfers between devices: 204 us -> 93.1 us  [on_device(): lax.all_to_all(part.reshape(seq_count, tok_dev, width), 'seq', split_axis...]
    pallas_call x0 -> x1, Pallas kernels: none -> 99.1 us  [attend(): pl.pallas_call(functools.partial(attend_kernel, per_group, head_block), o...]
    reduce_sum x8 -> x9, other arithmetic: 65.7 us -> 11.2 us  [the longest x1 7.91 us: on_device(): jnp.sum(source_part.astype(jnp.float32) * jnp.repeat(scaling, HDIM, axis=...]
    all_gather x1, waiting for transfers between devices: 0.01 us -> 52.5 us  [on_device(): all_queries = lax.all_gather(queries, 'seq', axis=0, tiled=True)]
    gather x5 -> x0, local copies, waits for them, and re-layouts: 36.9 us -> none  [the longest x2 17 us: on_device(): jnp.take(all_queries, query_rows, axis=0)]
    slice x4 -> x0, local copies, waits for them, and re-layouts: 34.7 us -> none  [the longest x1 16.3 us: on_device(): keys_all = jnp.concatenate([key_layout[group_id], own_keys], axis=0)]
  transfers between devices with their start and end apart: 4 -> 2, of which waited for: 1 -> 2; matrix products, arithmetic and copies ran while one was open for 30% -> 8% of each run, Pallas kernels for 0% -> 0%
where the time goes in v1:
time: 322 us; the launch traced here: 321 us
  waiting for transfers between devices  146 us (45%)
  Pallas kernels  99.1 us (31%)
  local copies, waits for them, and re-layouts  24.6 us (8%)
  other arithmetic  17.2 us (5%)
  blocking collectives  13.9 us (4%)
  between operations  13.5 us (4%)
  starting transfers between devices  7.17 us (2%)
    pallas_call x1, Pallas kernels, attend(): pl.pallas_call(functools.partial(attend_kernel, per_group, head_block), o...  99.1 us
    all_to_all x1, waiting for transfers between devices, on_device(): lax.all_to_all(part.reshape(seq_count, tok_dev, width), 'seq', split_axis...  93.1 us
    all_gather x1, waiting for transfers between devices, on_device(): all_queries = lax.all_gather(queries, 'seq', axis=0, tiled=True)  52.5 us
    reshape x1, local copies, waits for them, and re-layouts, on_device(): jnp.repeat(scaling, HDIM, axis=2)  12.9 us
    all_to_all x1, blocking collectives, on_device(): lax.all_to_all(lse.T.reshape(seq_count, tok_dev, heads), 'seq', split_axi...  10.2 us
    reduce_sum x1, other arithmetic, on_device(): jnp.sum(source_part.astype(jnp.float32) * jnp.repeat(scaling, HDIM, axis=...  7.91 us
    all_to_all x1, starting transfers between devices, on_device(): lax.all_to_all(part.reshape(seq_count, tok_dev, width), 'seq', split_axis...  7.17 us
    broadcast_in_dim x1, local copies, waits for them, and re-layouts, on_device(): jnp.repeat(scaling, HDIM, axis=2)  7.11 us
  transfers between devices with their start and end apart: 2, of which 2 were waited for; matrix products, arithmetic and copies ran while one was open for 8% of the time, Pallas kernels for 0%

profile of v1, /device:TPU:13, one launch (start us, length us, event | category | flops | bytes accessed | tf_op | source)
XLA Modules:
  0.0 321.2 jit_solution(12018052331025747732)
XLA Ops:
  6.5 1.3 fusion
  7.8 3.8 %all-reduce = (f32[64]{0:T(128)S(1)}, f32[64]{0:T(128)S(1)}) all-reduce(f32[64]{0:T(128)S(1)} %get-tuple-element.18, f32[64]{0:T(128)S(1)} %get-tuple-element.19), channel_id=1, replica_groups=mesh['seq'=16,'tp'=2] {'tp'}, use_global_device_ids=true, to_apply=%region_10.11 | all-reduce | flops 128 | bytes 1024 | tf_op jit(solution)/shard_map/psum | solution.py:230
  11.6 1.8 fusion.2
  13.6 0.9 select_reduce_fusion
  14.5 0.9 fusion.10
  15.6 0.9 convert_reduce_fusion.1
  16.5 0.7 iota_compare_fusion.2
  17.2 0.1 fusion.8.member_ref
  17.5 0.2 convert_reduce_fusion
  17.7 0.2 select_reduce_fusion.1
  17.8 1.1 fusion.5.nk_ref
  19.0 52.5 %all-gather.2.cloned.1.call-done = bf16[1024,2560]{1,0:T(8,128)(2,1)} async-done(((bf16[64,2560]{1,0:T(8,128)(2,1)}), bf16[1024,2560]{1,0:T(8,128)(2,1)}) %all-gather.2.cloned.1.call-update) | async-done | bytes 5242896 | tf_op jit(solution)/shard_map/all_gather | solution.py:235
  71.5 1.0 copy-done.1
  72.5 99.1 %attend.1 = (bf16[4,256,2560]{2,1,0:T(8,128)(2,1)S(1)}, f32[10,2,4,256]{3,2,1,0:T(4,128)S(1)}) custom-call(s32[2,16]{1,0:T(2,128)S(1)} %get-tuple-element.12.order_ref, s32[2,16]{1,0:T(2,128)S(1)} %get-tuple-element.11.limit_ref, s32[2,2]{1,0:T(2,128)S(1)} %pad_add_fusion.count_ref, s32[2,2]{1,0:T(2,128)S(1)} %fusion.8.member_ref, ...), custom_call_target="tpu_custom_call" | custom-call | tf_op jit(solution)/shard_map/attend/pallas_call | solution.py:137
  171.5 2.3 copy-done
  174.1 10.2 %all_to_all.10 = f32[16,1,1280]{2,1,0:T(1,128)S(1)} all-to-all(f32[16,1,1280]{2,1,0:T(1,128)S(1)} %reshape.185), channel_id=1, replica_groups=mesh['seq'=16,'tp'=2] {'seq'}, dimensions={0} | all-to-all | bytes 163840 | tf_op jit(solution)/shard_map/all_to_all | solution.py:249
  184.3 7.2 %all-to-all-start = ((bf16[16,64,2560]{2,1,0:T(8,128)(2,1)}), bf16[16,64,2560]{2,1,0:T(8,128)(2,1)}, u32[]{:S(2)}, u32[]{:S(2)}) async-start(bf16[16,64,2560]{2,1,0:T(8,128)(2,1)} %bitcast.21), calls=%async_computation | async-start | bytes 10485760 | tf_op jit(solution)/shard_map/all_to_all | solution.py:246
  191.5 0.5 broadcast.216
  192.0 0.8 reduce
  193.0 0.2 copy.27
  193.3 7.1 %broadcast_in_dim.111 = f32[16,64,20,128]{3,2,1,0:T(8,128)} broadcast(f32[16,64,20]{2,1,0:T(8,128)S(1)} %copy.27), dimensions={0,1,2} | broadcast | bytes 10567680 | tf_op jit(solution)/shard_map/broadcast_in_dim | solution.py:257
  200.4 12.9 %reshape.184 = f32[16,64,2560]{2,1,0:T(8,128)} reshape(f32[16,64,20,128]{3,2,1,0:T(8,128)} %broadcast_in_dim.111) | data formatting | bytes 20971520 | tf_op jit(solution)/shard_map/reshape | solution.py:257
  213.3 93.1 %all-to-all-done = bf16[16,64,2560]{2,1,0:T(8,128)(2,1)} async-done(((bf16[16,64,2560]{2,1,0:T(8,128)(2,1)}), bf16[16,64,2560]{2,1,0:T(8,128)(2,1)}, u32[]{:S(2)}, u32[]{:S(2)}) %all-to-all-start) | async-done | bytes 5242912 | tf_op jit(solution)/shard_map/all_to_all | solution.py:246
  306.4 7.9 %multiply_reduce_fusion = bf16[64,2560]{1,0:T(8,128)(2,1)} fusion(f32[16,64,2560]{2,1,0:T(8,128)} %reshape.184, bf16[16,64,2560]{2,1,0:T(8,128)(2,1)} %all-to-all-done), kind=kLoop, calls=%fused_computation | loop fusion | flops 7700480 | bytes 16056320 | tf_op jit(solution)/shard_map/reduce_sum | solution.py:255
  (24 shorter events, 1.0 us)
Async XLA Ops:
  6.5 65.0 %all-gather.2.cloned.1.call-start = ((), (), s32[]{:S(2)}) async-start(), calls=%async_computation.2 | async-start | bytes 5570560 | tf_op jit(solution)/shard_map/all_gather | solution.py:235
  71.5 1.0 copy-start.1
  171.5 2.3 copy-start
  184.3 122.1 %all-to-all-start = ((bf16[16,64,2560]{2,1,0:T(8,128)(2,1)}), bf16[16,64,2560]{2,1,0:T(8,128)(2,1)}, u32[]{:S(2)}, u32[]{:S(2)}) async-start(bf16[16,64,2560]{2,1,0:T(8,128)(2,1)} %bitcast.21), calls=%async_computation | async-start | bytes 10485760 | tf_op jit(solution)/shard_map/all_to_all | solution.py:246
Sparse Core Ops, SparseCore 0:
  13.6 57.8 all-gather.1

commit v2 on v1

--- a/solution.py
+++ b/solution.py
@@ -14,7 +14,8 @@
 EPSILON = 1e-06
 MASKED = -1e30
 FACTOR = math.log2(math.e) / math.sqrt(HDIM)
-BLOCK = 4
+BLOCKS = (8, 2)
+CHUNK_HEADS = 4
 
 
 def normalize(raw_rows, gain_row, sum_squares, full_width):
@@ -38,13 +39,15 @@
     nk_ref,
     nv_ref,
     o_ref,
-    lse_ref,
     top_ref,
     total_ref,
     acc_ref,
+    stat_ref,
 ):
+    step = pl.program_id(0)
     group = pl.program_id(1)
-    page_len = k_ref.shape[2]
+    wide = head_block * HDIM
+    stat_base = o_ref.shape[2] - HDIM
     own_rank = own_ref[group]
     full_pages = count_ref[group, 0]
     valid_pages = count_ref[group, 1]
@@ -78,84 +81,110 @@
         acc_ref[j] = mix_of(nv_ref[:, heads[j]], weights)
 
     def update(pages, masked, limit):
+        scores, values = [], []
         for j in range(head_block):
             keys = jnp.concatenate([k_ref[0, p, :, heads[j]] for p in pages], axis=0)
-            values = jnp.concatenate([v_ref[0, p, :, heads[j]] for p in pages], axis=0)
-            scores = scores_of(keys, j)
-            if masked:
-                allowed = lax.broadcasted_iota(jnp.int32, scores.shape, 0) < limit
-                scores = jnp.where(allowed, scores, MASKED)
-            before = top_ref[j]
-            top = jnp.maximum(before, jnp.max(scores, axis=0, keepdims=True))
-            weights = jnp.exp2(scores * FACTOR - top * FACTOR)
-            fade = jnp.exp2((before - top) * FACTOR)
-            top_ref[j] = top
-            total_ref[j] = total_ref[j] * fade + jnp.sum(weights, axis=0, keepdims=True)
-            acc_ref[j] = acc_ref[j] * fade + mix_of(values, weights)
-
-    blocks = full_pages // BLOCK
-
-    def full_step(b, _):
-        update([order_ref[group, b * BLOCK + i] for i in range(BLOCK)], False, None)
-        return 0
+            values.append(jnp.concatenate([v_ref[0, p, :, heads[j]] for p in pages], axis=0))
+            scores.append(scores_of(keys, j))
+        if masked:
+            allowed = lax.broadcasted_iota(jnp.int32, scores[0].shape, 0) < limit
+            scores = [jnp.where(allowed, each, MASKED) for each in scores]
+        before = [top_ref[j] for j in range(head_block)]
+        tops = [
+            jnp.maximum(old, jnp.max(each, axis=0, keepdims=True))
+            for old, each in zip(before, scores)
+        ]
+        weights = [jnp.exp2((each - top) * FACTOR) for each, top in zip(scores, tops)]
+        mixes = [mix_of(value, weight) for value, weight in zip(values, weights)]
+        for j in range(head_block):
+            fade = jnp.exp2((before[j] - tops[j]) * FACTOR)
+            top_ref[j] = tops[j]
+            total_ref[j] = total_ref[j] * fade + jnp.sum(weights[j], axis=0, keepdims=True)
+            acc_ref[j] = acc_ref[j] * fade + mixes[j]
+
+    done = 0
+    for size in BLOCKS:
+        count = (full_pages - done) // size
+
+        def full_step(b, _, size=size, done=done):
+            update([order_ref[group, done + b * size + i] for i in range(size)], False, None)
+            return 0
+
+        lax.fori_loop(0, count, full_step, 0)
+        done = done + count * size
 
     def tail_step(p, _):
         update([order_ref[group, p]], True, limit_ref[group, p])
         return 0
 
-    lax.fori_loop(0, blocks, full_step, 0)
-    lax.fori_loop(blocks * BLOCK, valid_pages, tail_step, 0)
+    lax.fori_loop(done, valid_pages, tail_step, 0)
+
+    @pl.when(step == 0)
+    def _():
+        stat_ref[group] = jnp.zeros(stat_ref.shape[1:], jnp.float32)
 
     for j in range(head_block):
         total = total_ref[j]
         some = total > 0.0
-        inverse = 1.0 / jnp.where(some, total, 1.0)
-        lse = jnp.where(some, top_ref[j] * FACTOR + jnp.log2(jnp.where(some, total, 1.0)), MASKED)
-        part = (acc_ref[j] * inverse).T.astype(jnp.bfloat16)
+        safe = jnp.where(some, total, 1.0)
+        lse = jnp.where(some, top_ref[j] * FACTOR + jnp.log2(safe), MASKED)
+        high = lse.astype(jnp.bfloat16).astype(jnp.float32)
+        stat_ref[group, pl.ds(step * head_block + j, 1), :] = high
+        stat_ref[group, pl.ds(HDIM // 2 + step * head_block + j, 1), :] = lse - high
+        part = (acc_ref[j] * (1.0 / safe)).T.astype(jnp.bfloat16)
+        columns = pl.ds(pl.multiple_of(step * wide + j * HDIM, HDIM), HDIM)
         for i, m in enumerate(members):
-            o_ref[m, :, heads[j]] = part[i * NEWTOK : (i + 1) * NEWTOK]
-            lse_ref[0, j, pl.ds(m, 1), :] = lse[:, i * NEWTOK : (i + 1) * NEWTOK]
-
-
-def attend(all_queries, cache_keys, cache_values, new_keys, v_new, order, limit, count, members, own):
-    tokens, width = all_queries.shape
+            o_ref[m, :, columns] = part[i * NEWTOK : (i + 1) * NEWTOK]
+
+    @pl.when(step == pl.num_programs(0) - 1)
+    def _():
+        stats = stat_ref[group].T.astype(jnp.bfloat16)
+        for i, m in enumerate(members):
+            o_ref[m, :, stat_base:] = stats[i * NEWTOK : (i + 1) * NEWTOK]
+
+
+def attend(first_head, chunk_queries, cache_keys, cache_values, new_keys, v_new, order, limit, count, members, own):
+    tokens, width = chunk_queries.shape
+    full_width = cache_keys.shape[2]
     requests = tokens // NEWTOK
     per_group = requests // GROUPS
     heads = width // HDIM
     head_block = 2 if heads % 2 == 0 else 1
     head_steps = heads // head_block
+    shift = first_head // head_block
     pages = cache_keys.shape[0] // GROUPS
     page_len = cache_keys.shape[1]
     tok_dev = new_keys.shape[0]
     lanes = per_group * NEWTOK
     wide = head_block * HDIM
-    keys = cache_keys.reshape(GROUPS, pages, page_len, width)
-    values = cache_values.reshape(GROUPS, pages, page_len, width)
+    keys = cache_keys.reshape(GROUPS, pages, page_len, full_width)
+    values = cache_values.reshape(GROUPS, pages, page_len, full_width)
     token_spec = pl.BlockSpec((requests, NEWTOK, wide), lambda h, g, *_: (0, 0, h))
-    cache_spec = pl.BlockSpec((1, pages, page_len, wide), lambda h, g, *_: (g, 0, 0, h))
-    own_spec = pl.BlockSpec((tok_dev, wide), lambda h, g, *_: (0, h))
-    part, lse = pl.pallas_call(
+    cache_spec = pl.BlockSpec((1, pages, page_len, wide), lambda h, g, *_: (g, 0, 0, h + shift))
+    own_spec = pl.BlockSpec((tok_dev, wide), lambda h, g, *_: (0, h + shift))
+    pairs = GROUPS * lanes * pages * page_len * heads
+    part = pl.pallas_call(
         functools.partial(attend_kernel, per_group, head_block),
-        out_shape=(
-            jax.ShapeDtypeStruct((requests, NEWTOK, width), jnp.bfloat16),
-            jax.ShapeDtypeStruct((head_steps, head_block, requests, NEWTOK), jnp.float32),
-        ),
+        out_shape=jax.ShapeDtypeStruct((requests, NEWTOK, width + HDIM), jnp.bfloat16),
         grid_spec=pltpu.PrefetchScalarGridSpec(
             num_scalar_prefetch=5,
             grid=(head_steps, GROUPS),
             in_specs=[token_spec, cache_spec, cache_spec, own_spec, own_spec],
-            out_specs=(
-                token_spec,
-                pl.BlockSpec((1, head_block, requests, NEWTOK), lambda h, g, *_: (h, 0, 0, 0)),
-            ),
+            out_specs=pl.BlockSpec((requests, NEWTOK, width + HDIM), lambda h, g, *_: (0, 0, 0)),
             scratch_shapes=[
                 pltpu.VMEM((head_block, 1, lanes), jnp.float32),
                 pltpu.VMEM((head_block, 1, lanes), jnp.float32),
                 pltpu.VMEM((head_block, HDIM, lanes), jnp.float32),
+                pltpu.VMEM((GROUPS, HDIM, lanes), jnp.float32),
             ],
         ),
         compiler_params=pltpu.CompilerParams(
             dimension_semantics=("arbitrary", "arbitrary"), vmem_limit_bytes=48 * 1024 * 1024
+        ),
+        cost_estimate=pl.CostEstimate(
+            flops=4 * pairs * HDIM,
+            bytes_accessed=2 * GROUPS * pages * page_len * width * 2,
+            transcendentals=pairs,
         ),
         name="attend",
     )(
@@ -164,13 +193,43 @@
         count,
         members,
         own,
-        all_queries.reshape(requests, NEWTOK, width),
+        chunk_queries.reshape(requests, NEWTOK, width),
         keys,
         values,
         new_keys,
         v_new,
     )
-    return part.reshape(tokens, width), lse.reshape(heads, tokens)
+    return part.reshape(tokens, width + HDIM)
+
+
+def merge_kernel(source_ref, out_ref):
+    sources, _, total_width = source_ref.shape
+    width = total_width - HDIM
+    half = HDIM // 2
+    lses = []
+    for s in range(sources):
+        stats = source_ref[s, :, width:].astype(jnp.float32)
+        lses.append(stats[:, :half] + stats[:, half:])
+    overall = functools.reduce(jnp.maximum, lses)
+    scaling = [jnp.exp2(each - overall) for each in lses]
+    inverse = 1.0 / functools.reduce(jnp.add, scaling)
+    for h in range(width // HDIM):
+        columns = slice(h * HDIM, (h + 1) * HDIM)
+        mixed = None
+        for s in range(sources):
+            term = source_ref[s, :, columns].astype(jnp.float32) * scaling[s][:, h : h + 1]
+            mixed = term if mixed is None else mixed + term
+        out_ref[:, columns] = (mixed * inverse[:, h : h + 1]).astype(jnp.bfloat16)
+
+
+def merge(source):
+    _, rows, total_width = source.shape
+    return pl.pallas_call(
+        merge_kernel,
+        out_shape=jax.ShapeDtypeStruct((rows, total_width - HDIM), jnp.bfloat16),
+        compiler_params=pltpu.CompilerParams(vmem_limit_bytes=32 * 1024 * 1024),
+        name="merge",
+    )(source)
 
 
 def plan_pages(page_table, cached_lengths, req_group, seq_index, pages_dev, page_len, tok_dev):
@@ -232,7 +291,14 @@
     )
     queries = normalize(q_raw, q_gain, query_sums, full_width)
     new_keys = normalize(k_raw, k_gain, key_sums, full_width)
-    all_queries = lax.all_gather(queries, "seq", axis=0, tiled=True)
+    chunk = CHUNK_HEADS if heads % CHUNK_HEADS == 0 else heads
+    starts = list(range(0, heads, chunk))
+    gathered = [
+        lax.all_gather(
+            queries[:, h * HDIM : (h + chunk) * HDIM], "seq", axis=0, tiled=True
+        )
+        for h in starts
+    ]
     plan = plan_pages(
         page_table,
         cached_lengths,
@@ -242,22 +308,18 @@
         cache_keys.shape[1],
         tok_dev,
     )
-    part, lse = attend(all_queries, cache_keys, cache_values, new_keys, v_new, *plan)
-    source_part = lax.all_to_all(
-        part.reshape(seq_count, tok_dev, width), "seq", split_axis=0, concat_axis=0, tiled=True
-    )
-    source_lse = lax.all_to_all(
-        lse.T.reshape(seq_count, tok_dev, heads), "seq", split_axis=0, concat_axis=0, tiled=True
-    )
-    overall = jnp.max(source_lse, axis=0)
-    scaling = jnp.exp2(source_lse - overall[None])
-    scaling = scaling / jnp.sum(scaling, axis=0)[None]
-    mixed = jnp.sum(
-        source_part.astype(jnp.float32)
-        * jnp.repeat(scaling, HDIM, axis=2),
-        axis=0,
-    )
-    return mixed.astype(jnp.bfloat16)
+    merged = []
+    for h, chunk_queries in zip(starts, gathered):
+        part = attend(h, chunk_queries, cache_keys, cache_values, new_keys, v_new, *plan)
+        source = lax.all_to_all(
+            part.reshape(seq_count, tok_dev, part.shape[1]),
+            "seq",
+            split_axis=0,
+            concat_axis=0,
+            tiled=True,
+        )
+        merged.append(merge(source))
+    return jnp.concatenate(merged, axis=1)
 
 
 def solution(mesh):

time: 322 us -> 402 us (1.25); the launches traced: 321 us -> 406 us
  waiting for transfers between devices: 146 us -> 249 us
  starting transfers between devices: 7.17 us -> 33 us
  local copies, waits for them, and re-layouts: 24.6 us -> 7.73 us
  other arithmetic: 17.2 us -> 4 us
  blocking collectives: 13.9 us -> 3.79 us
    all_gather x1 -> x5, waiting for transfers between devices: 52.5 us -> 222 us  [on_device(): lax.all_gather(queries[:, h * HDIM:(h + chunk) * HDIM], 'seq', axis=0, ti...]
    all_to_all x1 -> x5, waiting for transfers between devices: 93.1 us -> 24.7 us  [on_device(): lax.all_to_all(part.reshape(seq_count, tok_dev, part.shape[1]), 'seq', sp...]
    all_to_all x1 -> x5, starting transfers between devices: 7.17 us -> 32.7 us  [on_device(): lax.all_to_all(part.reshape(seq_count, tok_dev, part.shape[1]), 'seq', sp...]
    reshape x3 -> x0, local copies, waits for them, and re-layouts: 13.1 us -> none  [the longest x1 12.9 us: on_device(): jnp.repeat(scaling, HDIM, axis=2)]
    pallas_call x1 -> x5, Pallas kernels: 99.1 us -> 87.3 us  [attend(): pl.pallas_call(functools.partial(attend_kernel, per_group, head_block), o...]
    all_to_all x1 -> x0, blocking collectives: 10.2 us -> none  [on_device(): lax.all_to_all(lse.T.reshape(seq_count, tok_dev, heads), 'seq', split_axi...]
    pallas_call x0 -> x5, Pallas kernels: none -> 8.01 us  [merge(): pl.pallas_call(merge_kernel, out_shape=jax.ShapeDtypeStruct((rows, total_...]
    reduce_sum x2 -> x0, other arithmetic: 7.96 us -> none  [the longest x1 7.91 us: on_device(): jnp.sum(source_part.astype(jnp.float32) * jnp.repeat(scaling, HDIM, axis=...]
  transfers between devices with their start and end apart: 2 -> 10, of which waited for: 2 -> 6; matrix products, arithmetic and copies ran while one was open for 8% -> 0% of each run, Pallas kernels for 0% -> 19%
where the time goes in v2:
time: 402 us; the launch traced here: 406 us
  waiting for transfers between devices  249 us (62%)
  Pallas kernels  95.3 us (24%)
  starting transfers between devices  33 us (8%)
  between operations  13.3 us (3%)
  local copies, waits for them, and re-layouts  7.73 us (2%)
    all_gather x5, waiting for transfers between devices, on_device(): lax.all_gather(queries[:, h * HDIM:(h + chunk) * HDIM], 'seq', axis=0, ti...  222 us
    pallas_call x5, Pallas kernels, attend(): pl.pallas_call(functools.partial(attend_kernel, per_group, head_block), o...  87.3 us
    all_to_all x5, starting transfers between devices, on_device(): lax.all_to_all(part.reshape(seq_count, tok_dev, part.shape[1]), 'seq', sp...  32.7 us
    all_to_all x5, waiting for transfers between devices, on_device(): lax.all_to_all(part.reshape(seq_count, tok_dev, part.shape[1]), 'seq', sp...  24.7 us
  transfers between devices with their start and end apart: 10, of which 6 were waited for; matrix products, arithmetic and copies ran while one was open for 0% of the time, Pallas kernels for 19%

profile of v2, /device:TPU:13, one launch (start us, length us, event | category | flops | bytes accessed | tf_op | source)
XLA Modules:
  0.0 405.7 jit_solution(6643423469988659895)
XLA Ops:
  6.6 1.4 fusion
  8.0 3.8 all-reduce
  15.4 37.8 %all-gather.6.cloned.1.call-done = bf16[1024,512]{1,0:T(8,128)(2,1)} async-done(((bf16[64,512]{1,0:T(8,128)(2,1)}), bf16[1024,512]{1,0:T(8,128)(2,1)}) %all-gather.6.cloned.1.call-update) | async-done | bytes 1048592 | tf_op jit(solution)/shard_map/all_gather | solution.py:297
  53.2 1.2 copy-done.1
  54.5 17.4 %attend.5 = bf16[4,256,640]{2,1,0:T(8,128)(2,1)} custom-call(s32[2,16]{1,0:T(2,128)S(1)} %get-tuple-element.8.order_ref, s32[2,16]{1,0:T(2,128)S(1)} %get-tuple-element.7.limit_ref, s32[2,2]{1,0:T(2,128)S(1)} %pad_add_fusion.count_ref, s32[2,2]{1,0:T(2,128)S(1)} %fusion.6.member_ref, s32[2]{0:T(128)S(1)} %broadcast_add_fusion.own_ref, ...), custom_call_target="tpu_custom_call" | custom-call | flops 4294967296 | bytes 8388608 | tf_op jit(solution)/shard_map/attend/pallas_call | solution.py:166
  71.9 6.2 %all-to-all-start = ((bf16[16,64,640]{2,1,0:T(8,128)(2,1)}), bf16[16,64,640]{2,1,0:T(8,128)(2,1)S(1)}, u32[]{:S(2)}, u32[]{:S(2)}) async-start(bf16[16,64,640]{2,1,0:T(8,128)(2,1)} %bitcast.5), calls=%async_computation | async-start | bytes 2621440 | tf_op jit(solution)/shard_map/all_to_all | solution.py:314
  78.8 46.1 %all-gather.8.cloned.1.call-done = bf16[1024,512]{1,0:T(8,128)(2,1)} async-done(((bf16[64,512]{1,0:T(8,128)(2,1)}), bf16[1024,512]{1,0:T(8,128)(2,1)}) %all-gather.8.cloned.1.call-update) | async-done | bytes 1048592 | tf_op jit(solution)/shard_map/all_gather | solution.py:297
  124.9 1.2 copy-done.3
  126.2 17.5 %attend.6 = bf16[4,256,640]{2,1,0:T(8,128)(2,1)} custom-call(s32[2,16]{1,0:T(2,128)S(1)} %get-tuple-element.8.order_ref, s32[2,16]{1,0:T(2,128)S(1)} %get-tuple-element.7.limit_ref, s32[2,2]{1,0:T(2,128)S(1)} %pad_add_fusion.count_ref, s32[2,2]{1,0:T(2,128)S(1)} %fusion.6.member_ref, s32[2]{0:T(128)S(1)} %broadcast_add_fusion.own_ref, ...), custom_call_target="tpu_custom_call" | custom-call | flops 4294967296 | bytes 8388608 | tf_op jit(solution)/shard_map/attend/pallas_call | solution.py:166
  143.6 6.1 %all-to-all-start.1 = ((bf16[16,64,640]{2,1,0:T(8,128)(2,1)}), bf16[16,64,640]{2,1,0:T(8,128)(2,1)S(1)}, u32[]{:S(2)}, u32[]{:S(2)}) async-start(bf16[16,64,640]{2,1,0:T(8,128)(2,1)} %bitcast.7), calls=%async_computation.1 | async-start | bytes 2621440 | tf_op jit(solution)/shard_map/all_to_all | solution.py:314
  150.5 46.1 %all-gather.10.cloned.1.call-done = bf16[1024,512]{1,0:T(8,128)(2,1)} async-done(((bf16[64,512]{1,0:T(8,128)(2,1)}), bf16[1024,512]{1,0:T(8,128)(2,1)}) %all-gather.10.cloned.1.call-update) | async-done | bytes 1048592 | tf_op jit(solution)/shard_map/all_gather | solution.py:297
  196.6 1.2 copy-done.4
  197.8 17.5 %attend.7 = bf16[4,256,640]{2,1,0:T(8,128)(2,1)} custom-call(s32[2,16]{1,0:T(2,128)S(1)} %get-tuple-element.8.order_ref, s32[2,16]{1,0:T(2,128)S(1)} %get-tuple-element.7.limit_ref, s32[2,2]{1,0:T(2,128)S(1)} %pad_add_fusion.count_ref, s32[2,2]{1,0:T(2,128)S(1)} %fusion.6.member_ref, s32[2]{0:T(128)S(1)} %broadcast_add_fusion.own_ref, ...), custom_call_target="tpu_custom_call" | custom-call | flops 4294967296 | bytes 8388608 | tf_op jit(solution)/shard_map/attend/pallas_call | solution.py:166
  215.3 6.8 %all-to-all-start.2 = ((bf16[16,64,640]{2,1,0:T(8,128)(2,1)}), bf16[16,64,640]{2,1,0:T(8,128)(2,1)}, u32[]{:S(2)}, u32[]{:S(2)}) async-start(bf16[16,64,640]{2,1,0:T(8,128)(2,1)} %bitcast.9), calls=%async_computation.2 | async-start | bytes 2621440 | tf_op jit(solution)/shard_map/all_to_all | solution.py:314
  222.6 45.8 %all-gather.12.cloned.1.call-done = bf16[1024,512]{1,0:T(8,128)(2,1)} async-done(((bf16[64,512]{1,0:T(8,128)(2,1)}), bf16[1024,512]{1,0:T(8,128)(2,1)}) %all-gather.12.cloned.1.call-update) | async-done | bytes 1048592 | tf_op jit(solution)/shard_map/all_gather | solution.py:297
  269.7 17.4 %attend.8 = bf16[4,256,640]{2,1,0:T(8,128)(2,1)} custom-call(s32[2,16]{1,0:T(2,128)S(1)} %get-tuple-element.8.order_ref, s32[2,16]{1,0:T(2,128)S(1)} %get-tuple-element.7.limit_ref, s32[2,2]{1,0:T(2,128)S(1)} %pad_add_fusion.count_ref, s32[2,2]{1,0:T(2,128)S(1)} %fusion.6.member_ref, s32[2]{0:T(128)S(1)} %broadcast_add_fusion.own_ref, ...), custom_call_target="tpu_custom_call" | custom-call | flops 4294967296 | bytes 8388608 | tf_op jit(solution)/shard_map/attend/pallas_call | solution.py:166
  287.1 6.8 %all-to-all-start.3 = ((bf16[16,64,640]{2,1,0:T(8,128)(2,1)}), bf16[16,64,640]{2,1,0:T(8,128)(2,1)}, u32[]{:S(2)}, u32[]{:S(2)}) async-start(bf16[16,64,640]{2,1,0:T(8,128)(2,1)} %bitcast.11), calls=%async_computation.3 | async-start | bytes 2621440 | tf_op jit(solution)/shard_map/all_to_all | solution.py:314
  294.5 45.8 %all-gather.14.cloned.1.call-done = bf16[1024,512]{1,0:T(8,128)(2,1)} async-done(((bf16[64,512]{1,0:T(8,128)(2,1)}), bf16[1024,512]{1,0:T(8,128)(2,1)}) %all-gather.14.cloned.1.call-update) | async-done | bytes 1048592 | tf_op jit(solution)/shard_map/all_gather | solution.py:297
  341.5 17.4 %attend.9 = bf16[4,256,640]{2,1,0:T(8,128)(2,1)} custom-call(s32[2,16]{1,0:T(2,128)S(1)} %get-tuple-element.8.order_ref, s32[2,16]{1,0:T(2,128)S(1)} %get-tuple-element.7.limit_ref, s32[2,2]{1,0:T(2,128)S(1)} %pad_add_fusion.count_ref, s32[2,2]{1,0:T(2,128)S(1)} %fusion.6.member_ref, s32[2]{0:T(128)S(1)} %broadcast_add_fusion.own_ref, ...), custom_call_target="tpu_custom_call" | custom-call | flops 4294967296 | bytes 8388608 | tf_op jit(solution)/shard_map/attend/pallas_call | solution.py:166
  358.9 6.8 %all-to-all-start.4 = ((bf16[16,64,640]{2,1,0:T(8,128)(2,1)}), bf16[16,64,640]{2,1,0:T(8,128)(2,1)}, u32[]{:S(2)}, u32[]{:S(2)}) async-start(bf16[16,64,640]{2,1,0:T(8,128)(2,1)} %bitcast.13), calls=%async_computation.4 | async-start | bytes 2621440 | tf_op jit(solution)/shard_map/all_to_all | solution.py:314
  367.4 2.1 merge.7
  369.5 2.1 merge.8
  371.7 24.7 %all-to-all-done.4.source_ref = bf16[16,64,640]{2,1,0:T(8,128)(2,1)} async-done(((bf16[16,64,640]{2,1,0:T(8,128)(2,1)}), bf16[16,64,640]{2,1,0:T(8,128)(2,1)}, u32[]{:S(2)}, u32[]{:S(2)}) %all-to-all-start.4) | async-done | bytes 1310752 | tf_op jit(solution)/shard_map/all_to_all | solution.py:314
  396.4 2.1 merge.9
  (63 shorter events, 10.9 us)
Async XLA Ops:
  6.5 8.7 %copy-start.6 = (bf16[64,2560]{1,0:T(8,128)(2,1)S(1)}, bf16[64,2560]{1,0:T(8,128)(2,1)}, u32[]{:S(2)}) copy-start(bf16[64,2560]{1,0:T(8,128)(2,1)} %param.11) | copy-start | bytes 983044
  6.5 7.2 %copy-start.11 = (s32[4]{0:T(128)S(1)}, s32[4]{0:T(128)}, u32[]{:S(2)}) copy-start(s32[4]{0:T(128)} %param.19) | copy-start | bytes 52
  6.5 7.4 %copy-start.9 = (s32[2,256]{1,0:T(2,128)S(1)}, s32[2,256]{1,0:T(2,128)}, u32[]{:S(2)}) copy-start(s32[2,256]{1,0:T(2,128)} %param.17) | copy-start | bytes 6148
  6.5 7.6 %copy-start.10 = (s32[2]{0:T(128)S(1)}, s32[2]{0:T(128)}, u32[]{:S(2)}) copy-start(s32[2]{0:T(128)} %param.18) | copy-start | bytes 28
  6.5 8.7 %copy-start.8 = (f32[2560]{0:T(1024)S(1)}, f32[2560]{0:T(1024)}, u32[]{:S(2)}) copy-start(f32[2560]{0:T(1024)} %param.14) | copy-start | bytes 30724
  6.5 46.7 %copy-start = (bf16[64,2560]{1,0:T(8,128)(2,1)S(1)}, bf16[64,2560]{1,0:T(8,128)(2,1)}, u32[]{:S(2)}) copy-start(bf16[64,2560]{1,0:T(8,128)(2,1)} %nv_ref.9) | copy-start | bytes 983044
  6.6 46.7 %all-gather.6.cloned.1.call-start = ((), (), s32[]{:S(2)}) async-start(), calls=%async_computation.5 | async-start | bytes 1114112 | tf_op jit(solution)/shard_map/all_gather | solution.py:297
  53.2 1.2 copy-start.1
  71.9 71.7 %all-to-all-start = ((bf16[16,64,640]{2,1,0:T(8,128)(2,1)}), bf16[16,64,640]{2,1,0:T(8,128)(2,1)S(1)}, u32[]{:S(2)}, u32[]{:S(2)}) async-start(bf16[16,64,640]{2,1,0:T(8,128)(2,1)} %bitcast.5), calls=%async_computation | async-start | bytes 2621440 | tf_op jit(solution)/shard_map/all_to_all | solution.py:314
  78.1 46.9 %all-gather.8.cloned.1.call-start = ((), (), s32[]{:S(2)}) async-start(), calls=%async_computation.6 | async-start | bytes 1114112 | tf_op jit(solution)/shard_map/all_gather | solution.py:297
  124.9 1.2 copy-start.3
  143.6 71.7 %all-to-all-start.1 = ((bf16[16,64,640]{2,1,0:T(8,128)(2,1)}), bf16[16,64,640]{2,1,0:T(8,128)(2,1)S(1)}, u32[]{:S(2)}, u32[]{:S(2)}) async-start(bf16[16,64,640]{2,1,0:T(8,128)(2,1)} %bitcast.7), calls=%async_computation.1 | async-start | bytes 2621440 | tf_op jit(solution)/shard_map/all_to_all | solution.py:314
  149.8 46.8 %all-gather.10.cloned.1.call-start = ((), (), s32[]{:S(2)}) async-start(), calls=%async_computation.7 | async-start | bytes 1114112 | tf_op jit(solution)/shard_map/all_gather | solution.py:297
  196.6 1.2 copy-start.4
  215.3 71.8 %all-to-all-start.2 = ((bf16[16,64,640]{2,1,0:T(8,128)(2,1)}), bf16[16,64,640]{2,1,0:T(8,128)(2,1)}, u32[]{:S(2)}, u32[]{:S(2)}) async-start(bf16[16,64,640]{2,1,0:T(8,128)(2,1)} %bitcast.9), calls=%async_computation.2 | async-start | bytes 2621440 | tf_op jit(solution)/shard_map/all_to_all | solution.py:314
  222.1 46.4 %all-gather.12.cloned.1.call-start = ((), (), s32[]{:S(2)}) async-start(), calls=%async_computation.8 | async-start | bytes 1114112 | tf_op jit(solution)/shard_map/all_gather | solution.py:297
  268.4 1.2 copy-start.5
  287.1 71.8 %all-to-all-start.3 = ((bf16[16,64,640]{2,1,0:T(8,128)(2,1)}), bf16[16,64,640]{2,1,0:T(8,128)(2,1)}, u32[]{:S(2)}, u32[]{:S(2)}) async-start(bf16[16,64,640]{2,1,0:T(8,128)(2,1)} %bitcast.11), calls=%async_computation.3 | async-start | bytes 2621440 | tf_op jit(solution)/shard_map/all_to_all | solution.py:314
  293.9 46.4 %all-gather.14.cloned.1.call-start = ((), (), s32[]{:S(2)}) async-start(), calls=%async_computation.9 | async-start | bytes 1114112 | tf_op jit(solution)/shard_map/all_gather | solution.py:297
  340.3 1.2 copy-start.2
  358.9 37.5 %all-to-all-start.4 = ((bf16[16,64,640]{2,1,0:T(8,128)(2,1)}), bf16[16,64,640]{2,1,0:T(8,128)(2,1)}, u32[]{:S(2)}, u32[]{:S(2)}) async-start(bf16[16,64,640]{2,1,0:T(8,128)(2,1)} %bitcast.13), calls=%async_computation.4 | async-start | bytes 2621440 | tf_op jit(solution)/shard_map/all_to_all | solution.py:314
  371.7 26.9 %copy-start.7 = (bf16[64,2560]{1,0:T(8,128)(2,1)}, bf16[64,2560]{1,0:T(8,128)(2,1)S(1)}, u32[]{:S(2)}) copy-start(bf16[64,2560]{1,0:T(8,128)(2,1)S(1)} %constant_dynamic-update-slice_fusion.1) | copy-start | bytes 983044
Sparse Core Ops, SparseCore 0:
  13.8 39.3 all-gather.5
  81.1 43.8 all-gather.7
  152.8 43.7 all-gather.9
  224.8 43.6 all-gather.11
  296.6 43.6 all-gather.13
